TPU v7x, 128 devices: a whole 4x4x4 slice. The times are simulated.
128 devices in a mesh: ep: 16 (over x, z), tp: 8 (over y, core).
Axes of the slice: x: 4, y: 4, z: 4, core: 2. Of those that a mesh axis runs over, the one named last changes fastest.
Arguments:
- tokens: bfloat16 [2048, 4096], P('ep', 'tp'), may hold values from -6 to 6
- out_grad: bfloat16 [2048, 4096], P('ep', 'tp'), may hold values from -6 to 6
- routes: int32 [2048, 4], P('ep'), may hold values from 0 to 15, all different within a row; in each aligned block of 128 rows (0 to 127, 128 to 255, ...) at most 64 rows name the same one
- probs: bfloat16 [2048, 4], P('ep'), may hold values from 0.019897461 to 0.59765625
- w_in: bfloat16 [16, 2, 1536, 4096], P('ep', None, 'tp'), as said below
- w_out: bfloat16 [16, 1536, 4096], P('ep', 'tp'), as said below
Outputs:
- in_grad: bfloat16 [2048, 4096], P('ep', 'tp')
- grad_in: bfloat16 [16, 2, 1536, 4096], P('ep', None, 'tp')
- grad_out: bfloat16 [16, 1536, 4096], P('ep', 'tp')
Inputs may be any that keep to these rules, and one draw needn't show every extreme that they name: `routes`: each token names 4 different copies; within the tokens of one device (aligned blocks of 128 tokens) no copy is named more than 64 times, a bound that some block reaches. `w_in`: copies c and c + 8 hold equal weights. `w_out`: copies c and c + 8 hold equal weights.
All inputs are finite; a program needn't handle non-finite values.
Results may differ from a plain program's by a relative error of at most 0.02.
Values may be sent and summed in bfloat16 or wider, within the bound.
A program may use at most 128 MiB of HBM per device.

v0:
```python
import jax
import jax.numpy as jnp
from jax import lax
from jax.sharding import PartitionSpec as P


def partner(block, axis, apart):
    count = lax.axis_size(axis)
    route = []
    for low in range(count):
        high = low | 1 << apart
        if high != low and high < count:
            route += [(low, high), (high, low)]
    return lax.ppermute(block, axis, route)


def slot_tables(block_routes, copies, cap):
    flat = block_routes.reshape(-1)
    nrows = flat.shape[0]
    onehot = (flat[:, None] == jnp.arange(copies, dtype=jnp.int32)[None, :]).astype(jnp.int32)
    ranks = jnp.sum((jnp.cumsum(onehot, axis=0) - 1) * onehot, axis=1)
    slot = flat * cap + ranks
    source = (
        jnp.full((copies * cap,), nrows, jnp.int32).at[slot].set(jnp.arange(nrows, dtype=jnp.int32))
    )
    return (slot, source)


def body(tokens, out_grad, routes, probs, w_in, w_out):
    n_ep = lax.axis_size("ep")
    tok_dev, top = routes.shape
    nrows = tok_dev * top
    cap = 2 * nrows // n_ep
    slot, source = slot_tables(routes, n_ep, cap)
    valid = source < nrows
    local = jnp.minimum(source, nrows - 1)
    tok_index = local // top
    scale = jnp.where(valid, probs.reshape(-1)[local].astype(jnp.float32), 0.0)[:, None]
    full_x, full_g = (
        lax.all_gather(tokens, "tp", axis=1, tiled=True),
        lax.all_gather(out_grad, "tp", axis=1, tiled=True),
    )
    packed_x = jnp.where(valid[:, None], full_x[tok_index], jnp.zeros((), jnp.bfloat16))
    packed_g = (scale * full_g[tok_index].astype(jnp.float32)).astype(jnp.bfloat16)
    width = full_x.shape[1]
    send_x = packed_x.reshape(n_ep, cap, width)
    send_g = packed_g.reshape(n_ep, cap, width)
    recv_x, recv_g = (
        lax.all_to_all(send_x, "ep", split_axis=0, concat_axis=0, tiled=True),
        lax.all_to_all(send_g, "ep", split_axis=0, concat_axis=0, tiled=True),
    )
    width = recv_x.shape[2]
    rows_x = recv_x.reshape(n_ep * cap, width)
    rows_g = recv_g.reshape(n_ep * cap, width)
    w_gate = w_in[0, 0]
    w_up = w_in[0, 1]
    w_down = w_out[0]
    contract_last = (((1,), (1,)), ((), ()))
    a = lax.dot_general(rows_x, w_gate, contract_last, preferred_element_type=jnp.float32)
    b = lax.dot_general(rows_x, w_up, contract_last, preferred_element_type=jnp.float32)
    sig = jax.nn.sigmoid(a)
    silu = a * sig
    hidden = (silu * b).astype(jnp.bfloat16)
    dh = lax.dot_general(rows_g, w_down, contract_last, preferred_element_type=jnp.float32)
    da = (dh * b * sig * (1.0 + a * (1.0 - sig))).astype(jnp.bfloat16)
    db = (dh * silu).astype(jnp.bfloat16)
    partial_rows = jnp.dot(da, w_gate, preferred_element_type=jnp.float32)
    partial_rows = partial_rows + jnp.dot(db, w_up, preferred_element_type=jnp.float32)
    summed = lax.psum_scatter(
        partial_rows.reshape(n_ep, cap, width).astype(jnp.bfloat16),
        "tp",
        scatter_dimension=2,
        tiled=True,
    )
    back = lax.all_to_all(summed, "ep", split_axis=0, concat_axis=0, tiled=True)
    picked = back.reshape(n_ep * cap, back.shape[2])[slot]
    in_grad = jnp.sum(
        picked.astype(jnp.float32).reshape(tok_dev, top, back.shape[2]), axis=1
    ).astype(jnp.bfloat16)
    contract_rows = (((0,), (0,)), ((), ()))
    own_in = jnp.stack(
        [
            lax.dot_general(da, rows_x, contract_rows, preferred_element_type=jnp.float32),
            lax.dot_general(db, rows_x, contract_rows, preferred_element_type=jnp.float32),
        ]
    ).astype(jnp.bfloat16)[None]
    own_out = lax.dot_general(
        hidden, rows_g, contract_rows, preferred_element_type=jnp.float32
    ).astype(jnp.bfloat16)[None]
    half_bit = n_ep.bit_length() - 2
    other_in, other_out = partner((own_in, own_out), "ep", half_bit)
    grad_in = (own_in.astype(jnp.float32) + other_in.astype(jnp.float32)).astype(jnp.bfloat16)
    grad_out = (own_out.astype(jnp.float32) + other_out.astype(jnp.float32)).astype(jnp.bfloat16)
    return (in_grad, grad_in, grad_out)


def solution(mesh):
    return jax.shard_map(
        body,
        mesh=mesh,
        in_specs=(
            P("ep", "tp"),
            P("ep", "tp"),
            P("ep", None),
            P("ep", None),
            P("ep", None, "tp", None),
            P("ep", "tp", None),
        ),
        out_specs=(P("ep", "tp"), P("ep", None, "tp", None), P("ep", "tp", None)),
        check_vma=False,
    )
```

profile of v0, /device:TPU:0, one launch (start us, length us, event | category | flops | bytes accessed | tf_op | source)
XLA Modules:
  0.0 534.7 jit_solution(16174911186118901653)
XLA Ops:
  7.9 0.8 copy.10
  8.9 1.2 reduce-window.6
  11.3 0.8 copy.13
  12.3 2.4 scatter_custom_fusion
  14.8 6.8 %gather_fusion = bf16[1024]{0:T(1024)(128)(2,1)S(1)} fusion(bf16[512]{0:T(512)(128)(2,1)S(1)} %reshape.144, s32[1024]{0:T(1024)S(1)} %get-tuple-element.7), kind=kCustom, calls=%fused_computation | custom fusion | bytes 8192 | tf_op jit(solution)/shard_map/gather | solution.py:38
  21.7 13.9 %all-gather.5.cloned.1.call-done = bf16[128,4096]{1,0:T(8,128)(2,1)} async-done(((bf16[128,512]{1,0:T(8,128)(2,1)}), bf16[128,4096]{1,0:T(8,128)(2,1)}) %all-gather.5.cloned.1.call-update) | async-done | bytes 1048592 | tf_op jit(solution)/shard_map/all_gather | solution.py:40
  35.6 16.4 %gather_fusion.2 = bf16[1024,4096]{1,0:T(8,128)(2,1)} fusion(bf16[128,4096]{1,0:T(8,128)(2,1)} %all-gather.5.cloned.1.call-done, s32[1024]{0:T(1024)S(1)} %get-tuple-element.8), kind=kCustom, calls=%fused_computation.2 | custom fusion | bytes 16781312 | tf_op jit(solution)/shard_map/gather | solution.py:43
  52.0 7.2 %broadcast_select_fusion = bf16[16,64,4096]{2,1,0:T(8,128)(2,1)} fusion(bf16[16,64,4096]{2,1,0:T(8,128)(2,1)} %bitcast.56, pred[16,64]{1,0:T(8,128)(4,1)S(1)} %broadcast_in_dim.35), kind=kLoop, calls=%fused_computation.8 | loop fusion | flops 4194304 | bytes 16778240 | tf_op jit(solution)/shard_map/jit(_where)/select_n | solution.py:43
  59.2 7.0 %all-to-all-start.1 = ((bf16[16,64,4096]{2,1,0:T(8,128)(2,1)}), bf16[16,64,4096]{2,1,0:T(8,128)(2,1)}, u32[]{:S(2)}, u32[]{:S(2)}) async-start(bf16[16,64,4096]{2,1,0:T(8,128)(2,1)} %broadcast_select_fusion), calls=%async_computation.1 | async-start | bytes 16777216 | tf_op jit(solution)/shard_map/all_to_all | solution.py:49
  67.1 25.2 %all-gather.3.cloned.1.call-done = bf16[128,4096]{1,0:T(8,128)(2,1)} async-done(((bf16[128,512]{1,0:T(8,128)(2,1)}), bf16[128,4096]{1,0:T(8,128)(2,1)}) %all-gather.3.cloned.1.call-update) | async-done | bytes 1048592 | tf_op jit(solution)/shard_map/all_gather | solution.py:41
  92.3 16.4 %gather_fusion.1 = bf16[1024,4096]{1,0:T(8,128)(2,1)} fusion(bf16[128,4096]{1,0:T(8,128)(2,1)} %all-gather.3.cloned.1.call-done, s32[1024]{0:T(1024)S(1)} %get-tuple-element.8), kind=kCustom, calls=%fused_computation.1 | custom fusion | bytes 16781312 | tf_op jit(solution)/shard_map/gather | solution.py:44
  108.7 10.0 %fusion = bf16[16,64,4096]{2,1,0:T(8,128)(2,1)} fusion(bf16[16,64,4096]{2,1,0:T(8,128)(2,1)} %bitcast.57, f32[16,64]{1,0:T(8,128)S(1)} %mul.55), kind=kLoop, calls=%fused_computation.6 | loop fusion | flops 12582912 | bytes 16781312 | tf_op jit(solution)/shard_map/convert_element_type | solution.py:44
  118.7 93.8 %all-to-all-done.1 = bf16[16,64,4096]{2,1,0:T(8,128)(2,1)} async-done(((bf16[16,64,4096]{2,1,0:T(8,128)(2,1)}), bf16[16,64,4096]{2,1,0:T(8,128)(2,1)}, u32[]{:S(2)}, u32[]{:S(2)}) %all-to-all-start.1) | async-done | bytes 8388640 | tf_op jit(solution)/shard_map/all_to_all | solution.py:49
  212.5 11.8 %all-to-all-start = ((bf16[16,64,4096]{2,1,0:T(8,128)(2,1)}), bf16[16,64,4096]{2,1,0:T(8,128)(2,1)}, u32[]{:S(2)}, u32[]{:S(2)}) async-start(bf16[16,64,4096]{2,1,0:T(8,128)(2,1)} %fusion), calls=%async_computation | async-start | bytes 16777216 | tf_op jit(solution)/shard_map/all_to_all | solution.py:50
  224.5 6.8 %fusion.6 = f32[1024,192]{0,1:T(8,128)S(1)} fusion(bf16[1024,4096]{1,0:T(8,128)(2,1)} %bitcast.7, bf16[1,2,192,4096]{3,2,1,0:T(8,128)(2,1)} %param.10), kind=kOutput, calls=%fused_computation.20 | convolution fusion | flops 1610612736 | bytes 10747904 | tf_op jit(solution)/shard_map/dot_general | solution.py:59
  231.4 7.2 %fusion.9 = f32[1024,192]{0,1:T(8,128)} fusion(bf16[1024,4096]{1,0:T(8,128)(2,1)} %bitcast.7, bf16[1,2,192,4096]{3,2,1,0:T(8,128)(2,1)S(1)} %copy-done.3), kind=kOutput, calls=%fused_computation.23 | convolution fusion | flops 1610612736 | bytes 10747904 | tf_op jit(solution)/shard_map/dot_general | solution.py:60
  238.5 119.4 %all-to-all-done = bf16[16,64,4096]{2,1,0:T(8,128)(2,1)} async-done(((bf16[16,64,4096]{2,1,0:T(8,128)(2,1)}), bf16[16,64,4096]{2,1,0:T(8,128)(2,1)}, u32[]{:S(2)}, u32[]{:S(2)}) %all-to-all-start) | async-done | bytes 8388640 | tf_op jit(solution)/shard_map/all_to_all | solution.py:50
  357.9 6.7 %multiply_convert_fusion.1 = (bf16[1024,192]{0,1:T(8,128)(2,1)S(1)}, bf16[1024,192]{0,1:T(8,128)(2,1)S(1)}) fusion(f32[1024,192]{0,1:T(8,128)S(1)} %fusion.6, f32[1024,192]{0,1:T(8,128)} %fusion.9, bf16[1024,4096]{1,0:T(8,128)(2,1)} %bitcast.4, bf16[1,192,4096]{2,1,0:T(8,128)(2,1)S(1)} %copy-done), kind=kOutput, calls=%fused_computation.32 | convolution fusion | flops 1613168640 | bytes 12320768 | tf_op jit(solution)/shard_map/dot_general | solution.py:64
  364.6 8.1 %fusion.4 = f32[1024,4096]{1,0:T(8,128)} fusion(bf16[1024,192]{0,1:T(8,128)(2,1)S(1)} %get-tuple-element.6, bf16[1,2,192,4096]{3,2,1,0:T(8,128)(2,1)S(1)} %copy-done.4), kind=kOutput, calls=%fused_computation.18 | convolution fusion | flops 1610612736 | bytes 18743296 | tf_op jit(solution)/shard_map/dot_general | solution.py:67
  372.8 11.4 %add_convert_fusion = bf16[1024,4096]{1,0:T(8,128)(2,1)} fusion(f32[1024,4096]{1,0:T(8,128)} %fusion.4, bf16[1024,192]{0,1:T(8,128)(2,1)S(1)} %get-tuple-element.5, bf16[1,2,192,4096]{3,2,1,0:T(8,128)(2,1)S(1)} %copy-done.4), kind=kOutput, calls=%fused_computation.7 | convolution fusion | flops 1619001344 | bytes 27131904 | tf_op jit(solution)/shard_map/dot_general | solution.py:68
  384.2 5.4 %fusion.1 = bf16[1,1,192,4096]{3,2,1,0:T(8,128)(2,1)S(1)} fusion(bf16[1024,192]{0,1:T(8,128)(2,1)S(1)} %get-tuple-element.6, bf16[1024,4096]{1,0:T(8,128)(2,1)} %bitcast.7), kind=kOutput, calls=%fused_computation.13 | convolution fusion | flops 1611399168 | bytes 10354688 | tf_op jit(solution)/shard_map/dot_general | solution.py:83
  389.7 5.8 %fusion.2 = bf16[1,1,192,4096]{3,2,1,0:T(8,128)(2,1)S(1)} fusion(bf16[1024,192]{0,1:T(8,128)(2,1)S(1)} %get-tuple-element.5, bf16[1024,4096]{1,0:T(8,128)(2,1)} %bitcast.7), kind=kOutput, calls=%fused_computation.14 | convolution fusion | flops 1611399168 | bytes 10354688 | tf_op jit(solution)/shard_map/dot_general | solution.py:84
  395.4 1.9 pad_maximum_fusion
  397.6 5.3 fusion.3
  402.9 3.7 collective-permute-start.1
  406.6 92.6 %collective-permute-done.1 = bf16[1,192,4096]{2,1,0:T(8,128)(2,1)S(1)} collective-permute-done((bf16[1,192,4096]{2,1,0:T(8,128)(2,1)S(1)}, bf16[1,192,4096]{2,1,0:T(8,128)(2,1)S(1)}, u32[]{:S(2)}, u32[]{:S(2)}) %collective-permute-start.1) | collective-permute-done | bytes 1572896 | tf_op jit(solution)/shard_map/ppermute | solution.py:14
  499.2 1.7 add_convert_fusion.2
  500.9 9.9 %all-to-all-start.2 = ((bf16[16,64,512]{2,1,0:T(8,128)(2,1)}), bf16[16,64,512]{2,1,0:T(8,128)(2,1)S(1)}, u32[]{:S(2)}, u32[]{:S(2)}) async-start(bf16[16,64,512]{2,1,0:T(8,128)(2,1)} %reduce-scatter.2.cloned.1.call-done), calls=%async_computation.3 | async-start | bytes 2097152 | tf_op jit(solution)/shard_map/all_to_all | solution.py:75
  510.8 5.8 %add_convert_fusion.1 = bf16[1,2,192,4096]{3,2,1,0:T(8,128)(2,1)} fusion(bf16[1,2,192,4096]{3,2,1,0:T(8,128)(2,1)} %collective-permute-done, bf16[1,1,192,4096]{3,2,1,0:T(8,128)(2,1)} %copy-done.2, bf16[1,1,192,4096]{3,2,1,0:T(8,128)(2,1)} %copy-done.1), kind=kLoop, calls=%fused_computation.9 | loop fusion | flops 7864320 | bytes 9437184 | tf_op jit(solution)/shard_map/convert_element_type | solution.py:92
  516.6 8.2 %all-to-all-done.2 = bf16[16,64,512]{2,1,0:T(8,128)(2,1)S(1)} async-done(((bf16[16,64,512]{2,1,0:T(8,128)(2,1)}), bf16[16,64,512]{2,1,0:T(8,128)(2,1)S(1)}, u32[]{:S(2)}, u32[]{:S(2)}) %all-to-all-start.2) | async-done | bytes 1048608 | tf_op jit(solution)/shard_map/all_to_all | solution.py:75
  524.7 2.0 gather_fusion.3
  526.8 1.3 reduce_sum.25
  (40 shorter events, 3.9 us)
Async XLA Ops:
  7.2 350.7 %copy-start = (bf16[1,192,4096]{2,1,0:T(8,128)(2,1)S(1)}, bf16[1,192,4096]{2,1,0:T(8,128)(2,1)}, u32[]{:S(2)}) copy-start(bf16[1,192,4096]{2,1,0:T(8,128)(2,1)} %param.11) | copy-start | bytes 4718596
  7.2 28.4 %all-gather.5.cloned.1.call-start = ((), (), s32[]{:S(2)}) async-start(), calls=%async_computation.5 | async-start | bytes 1179648 | tf_op jit(solution)/shard_map/all_gather | solution.py:40
  59.2 153.3 %all-to-all-start.1 = ((bf16[16,64,4096]{2,1,0:T(8,128)(2,1)}), bf16[16,64,4096]{2,1,0:T(8,128)(2,1)}, u32[]{:S(2)}, u32[]{:S(2)}) async-start(bf16[16,64,4096]{2,1,0:T(8,128)(2,1)} %broadcast_select_fusion), calls=%async_computation.1 | async-start | bytes 16777216 | tf_op jit(solution)/shard_map/all_to_all | solution.py:49
  66.3 26.0 %all-gather.3.cloned.1.call-start = ((), (), s32[]{:S(2)}) async-start(), calls=%async_computation.4 | async-start | bytes 1179648 | tf_op jit(solution)/shard_map/all_gather | solution.py:41
  212.5 145.4 %all-to-all-start = ((bf16[16,64,4096]{2,1,0:T(8,128)(2,1)}), bf16[16,64,4096]{2,1,0:T(8,128)(2,1)}, u32[]{:S(2)}, u32[]{:S(2)}) async-start(bf16[16,64,4096]{2,1,0:T(8,128)(2,1)} %fusion), calls=%async_computation | async-start | bytes 16777216 | tf_op jit(solution)/shard_map/all_to_all | solution.py:50
  224.3 276.6 %reduce-scatter.2.cloned.1.call-start = ((), (), s32[]{:S(2)}) async-start(), calls=%async_computation.6 | async-start | bytes 9437184 | tf_op jit(solution)/shard_map/reduce_scatter | solution.py:69
  224.5 6.9 %copy-start.3 = (bf16[1,2,192,4096]{3,2,1,0:T(8,128)(2,1)S(1)}, bf16[1,2,192,4096]{3,2,1,0:T(8,128)(2,1)}, u32[]{:S(2)}) copy-start(bf16[1,2,192,4096]{3,2,1,0:T(8,128)(2,1)} %param.10) | copy-start | bytes 9437188
  357.9 6.7 %copy-start.4 = (bf16[1,2,192,4096]{3,2,1,0:T(8,128)(2,1)S(1)}, bf16[1,2,192,4096]{3,2,1,0:T(8,128)(2,1)}, u32[]{:S(2)}) copy-start(bf16[1,2,192,4096]{3,2,1,0:T(8,128)(2,1)} %param.10) | copy-start | bytes 9437188
  389.6 5.8 %copy-start.1 = (bf16[1,1,192,4096]{3,2,1,0:T(8,128)(2,1)}, bf16[1,1,192,4096]{3,2,1,0:T(8,128)(2,1)S(1)}, u32[]{:S(2)}) copy-start(bf16[1,1,192,4096]{3,2,1,0:T(8,128)(2,1)S(1)} %fusion.1) | copy-start | bytes 4718596
  395.4 2.2 copy-start.2
  395.4 2.2 copy-start.5
  397.6 113.2 %collective-permute-start = (bf16[1,2,192,4096]{3,2,1,0:T(8,128)(2,1)}, bf16[1,2,192,4096]{3,2,1,0:T(8,128)(2,1)}, u32[]{:S(2)}, u32[]{:S(2)}) collective-permute-start(bf16[1,2,192,4096]{3,2,1,0:T(8,128)(2,1)} %pad_maximum_fusion), channel_id=1, source_target_pairs={{0,64},{64,0},{8,72},{72,8},{16,80},{80,16},{24,88},{88,24},{32,96... | collective-permute-start | bytes 9437192 | tf_op jit(solution)/shard_map/ppermute | solution.py:14
  402.9 96.3 %collective-permute-start.1 = (bf16[1,192,4096]{2,1,0:T(8,128)(2,1)S(1)}, bf16[1,192,4096]{2,1,0:T(8,128)(2,1)S(1)}, u32[]{:S(2)}, u32[]{:S(2)}) collective-permute-start(bf16[1,192,4096]{2,1,0:T(8,128)(2,1)S(1)} %fusion.3), channel_id=1, source_target_pairs={{0,64},{64,0},{8,72},{72,8},{16,80},{80,16},{24,88},{88,24},{32,96... | collective-permute-start | bytes 4718600 | tf_op jit(solution)/shard_map/ppermute | solution.py:14
  500.9 23.9 %all-to-all-start.2 = ((bf16[16,64,512]{2,1,0:T(8,128)(2,1)}), bf16[16,64,512]{2,1,0:T(8,128)(2,1)S(1)}, u32[]{:S(2)}, u32[]{:S(2)}) async-start(bf16[16,64,512]{2,1,0:T(8,128)(2,1)} %reduce-scatter.2.cloned.1.call-done), calls=%async_computation.3 | async-start | bytes 2097152 | tf_op jit(solution)/shard_map/all_to_all | solution.py:75
Sparse Core Ops, SparseCore 0:
  9.7 25.8 all-gather.4
  68.8 23.4 all-gather.2
  384.3 54.3 reduce-scatter.1
where the time goes:
time: 535 us
  waiting for transfers between devices  354 us (66%)
  matrix products  56.7 us (11%)
  local copies, waits for them, and re-layouts  47 us (9%)
  starting transfers between devices  32.6 us (6%)
  other arithmetic  30 us (6%)
  between operations  14 us (3%)
    all_to_all x1, waiting for transfers between devices, body(): lax.all_to_all(send_g, 'ep', split_axis=0, concat_axis=0, tiled=True)  119 us
    all_to_all x1, waiting for transfers between devices, body(): lax.all_to_all(send_x, 'ep', split_axis=0, concat_axis=0, tiled=True)  93.8 us
    ppermute x2, waiting for transfers between devices, partner(): return lax.ppermute(block, axis, route)  92.6 us
    all_gather x1, waiting for transfers between devices, body(): lax.all_gather(out_grad, 'tp', axis=1, tiled=True)  25.2 us
    gather x1, local copies, waits for them, and re-layouts, body(): full_g[tok_index].astype(jnp.float32)  16.4 us
    gather x1, local copies, waits for them, and re-layouts, body(): full_x[tok_index]  16.4 us
    all_gather x1, waiting for transfers between devices, body(): lax.all_gather(tokens, 'tp', axis=1, tiled=True)  13.9 us
    all_to_all x1, starting transfers between devices, body(): lax.all_to_all(send_g, 'ep', split_axis=0, concat_axis=0, tiled=True)  11.8 us
  transfers between devices with their start and end apart: 8, of which 6 were waited for; matrix products, arithmetic and copies ran while one was open for 15% of the time, Pallas kernels for 0%

commit v1 on v0

--- a/solution.py
+++ b/solution.py
@@ -2,6 +2,12 @@
 import jax.numpy as jnp
 from jax import lax
 from jax.sharding import PartitionSpec as P
+
+
+def load_gates(panel, a_name="tp"):
+    y2 = jnp.concatenate(lax.axis_size(a_name) * [panel], 1)
+    s_next = lax.all_to_all(y2, axis_name=a_name, concat_axis=1, split_axis=1, tiled=True)
+    return s_next
 
 
 def partner(block, axis, apart):
@@ -36,10 +42,7 @@
     local = jnp.minimum(source, nrows - 1)
     tok_index = local // top
     scale = jnp.where(valid, probs.reshape(-1)[local].astype(jnp.float32), 0.0)[:, None]
-    full_x, full_g = (
-        lax.all_gather(tokens, "tp", axis=1, tiled=True),
-        lax.all_gather(out_grad, "tp", axis=1, tiled=True),
-    )
+    full_x, full_g = (load_gates(tokens), lax.all_gather(out_grad, "tp", axis=1, tiled=True))
     packed_x = jnp.where(valid[:, None], full_x[tok_index], jnp.zeros((), jnp.bfloat16))
     packed_g = (scale * full_g[tok_index].astype(jnp.float32)).astype(jnp.bfloat16)
     width = full_x.shape[1]

time: 535 us -> 518 us (0.968)
  the two profiles are of different devices: /device:TPU:0 before, /device:TPU:16 now
where the time goes in v1:
time: 518 us
  waiting for transfers between devices  341 us (66%)
  matrix products  56.8 us (11%)
  local copies, waits for them, and re-layouts  42 us (8%)
  starting transfers between devices  33.9 us (7%)
  other arithmetic  29.3 us (6%)
  between operations  14.4 us (3%)
    all_to_all x1, waiting for transfers between devices, body(): lax.all_to_all(send_g, 'ep', split_axis=0, concat_axis=0, tiled=True)  119 us
    all_to_all x1, waiting for transfers between devices, body(): lax.all_to_all(send_x, 'ep', split_axis=0, concat_axis=0, tiled=True)  94 us
    ppermute x2, waiting for transfers between devices, partner(): return lax.ppermute(block, axis, route)  92.2 us
    all_gather x1, waiting for transfers between devices, body(): lax.all_gather(out_grad, 'tp', axis=1, tiled=True)  26 us
    gather x1, local copies, waits for them, and re-layouts, body(): full_g[tok_index].astype(jnp.float32)  16.4 us
    dot_general x1, matrix products, body(): jnp.dot(db, w_up, preferred_element_type=jnp.float32)  11.4 us
  transfers between devices with their start and end apart: 8, of which 6 were waited for; matrix products, arithmetic and copies ran while one was open for 15% of the time, Pallas kernels for 0%

profile of v1, /device:TPU:16, one launch (start us, length us, event | category | flops | bytes accessed | tf_op | source)
XLA Modules:
  0.0 517.6 jit_solution(3885076570865866522)
XLA Ops:
  8.6 1.3 copy.33
  9.9 4.8 all-to-all-start.1
  15.0 1.2 reduce-window.6
  17.1 2.4 scatter_custom_fusion
  19.5 6.8 %gather_fusion = bf16[1024]{0:T(1024)(128)(2,1)S(1)} fusion(bf16[512]{0:T(512)(128)(2,1)S(1)} %reshape.146, s32[1024]{0:T(1024)S(1)} %get-tuple-element.7), kind=kCustom, calls=%fused_computation | custom fusion | bytes 8192 | tf_op jit(solution)/shard_map/gather | solution.py:44
  28.5 1.3 copy.36
  29.8 7.8 %gather_fusion.2 = bf16[1024,4096]{1,0:T(8,128)(2,1)} fusion(bf16[128,4096]{1,0:T(8,128)(2,1)S(1)} %bitcast.58, s32[1024]{0:T(1024)S(1)} %get-tuple-element.8), kind=kCustom, calls=%fused_computation.2 | custom fusion | bytes 16781312 | tf_op jit(solution)/shard_map/gather | solution.py:46
  37.6 7.2 %broadcast_select_fusion = bf16[16,64,4096]{2,1,0:T(8,128)(2,1)} fusion(bf16[16,64,4096]{2,1,0:T(8,128)(2,1)} %bitcast.60, pred[16,64]{1,0:T(8,128)(4,1)S(1)} %broadcast_in_dim.35), kind=kLoop, calls=%fused_computation.8 | loop fusion | flops 4194304 | bytes 16778240 | tf_op jit(solution)/shard_map/jit(_where)/select_n | solution.py:46
  44.8 7.9 %all-to-all-start.2 = ((bf16[16,64,4096]{2,1,0:T(8,128)(2,1)}), bf16[16,64,4096]{2,1,0:T(8,128)(2,1)}, u32[]{:S(2)}, u32[]{:S(2)}) async-start(bf16[16,64,4096]{2,1,0:T(8,128)(2,1)} %broadcast_select_fusion), calls=%async_computation.2 | async-start | bytes 16777216 | tf_op jit(solution)/shard_map/all_to_all | solution.py:52
  53.6 26.0 %all-gather.2.cloned.1.call-done = bf16[128,4096]{1,0:T(8,128)(2,1)} async-done(((bf16[128,512]{1,0:T(8,128)(2,1)}), bf16[128,4096]{1,0:T(8,128)(2,1)}) %all-gather.2.cloned.1.call-update) | async-done | bytes 1048592 | tf_op jit(solution)/shard_map/all_gather | solution.py:45
  79.5 16.4 %gather_fusion.1 = bf16[1024,4096]{1,0:T(8,128)(2,1)} fusion(bf16[128,4096]{1,0:T(8,128)(2,1)} %all-gather.2.cloned.1.call-done, s32[1024]{0:T(1024)S(1)} %get-tuple-element.8), kind=kCustom, calls=%fused_computation.1 | custom fusion | bytes 16781312 | tf_op jit(solution)/shard_map/gather | solution.py:47
  96.0 10.0 %fusion = bf16[16,64,4096]{2,1,0:T(8,128)(2,1)} fusion(bf16[16,64,4096]{2,1,0:T(8,128)(2,1)} %bitcast.61, f32[16,64]{1,0:T(8,128)S(1)} %mul.55), kind=kLoop, calls=%fused_computation.6 | loop fusion | flops 12582912 | bytes 16781312 | tf_op jit(solution)/shard_map/convert_element_type | solution.py:47
  106.0 94.0 %all-to-all-done.2 = bf16[16,64,4096]{2,1,0:T(8,128)(2,1)} async-done(((bf16[16,64,4096]{2,1,0:T(8,128)(2,1)}), bf16[16,64,4096]{2,1,0:T(8,128)(2,1)}, u32[]{:S(2)}, u32[]{:S(2)}) %all-to-all-start.2) | async-done | bytes 8388640 | tf_op jit(solution)/shard_map/all_to_all | solution.py:52
  200.0 8.4 %all-to-all-start = ((bf16[16,64,4096]{2,1,0:T(8,128)(2,1)}), bf16[16,64,4096]{2,1,0:T(8,128)(2,1)}, u32[]{:S(2)}, u32[]{:S(2)}) async-start(bf16[16,64,4096]{2,1,0:T(8,128)(2,1)} %fusion), calls=%async_computation | async-start | bytes 16777216 | tf_op jit(solution)/shard_map/all_to_all | solution.py:53
  208.6 6.8 %fusion.6 = f32[1024,192]{0,1:T(8,128)S(1)} fusion(bf16[1024,4096]{1,0:T(8,128)(2,1)} %bitcast.8, bf16[1,2,192,4096]{3,2,1,0:T(8,128)(2,1)} %param.10), kind=kOutput, calls=%fused_computation.20 | convolution fusion | flops 1610612736 | bytes 10747904 | tf_op jit(solution)/shard_map/dot_general | solution.py:62
  215.5 7.2 %fusion.9 = f32[1024,192]{0,1:T(8,128)} fusion(bf16[1024,4096]{1,0:T(8,128)(2,1)} %bitcast.8, bf16[1,2,192,4096]{3,2,1,0:T(8,128)(2,1)S(1)} %copy-done.4), kind=kOutput, calls=%fused_computation.23 | convolution fusion | flops 1610612736 | bytes 10747904 | tf_op jit(solution)/shard_map/dot_general | solution.py:63
  222.6 119.4 %all-to-all-done = bf16[16,64,4096]{2,1,0:T(8,128)(2,1)} async-done(((bf16[16,64,4096]{2,1,0:T(8,128)(2,1)}), bf16[16,64,4096]{2,1,0:T(8,128)(2,1)}, u32[]{:S(2)}, u32[]{:S(2)}) %all-to-all-start) | async-done | bytes 8388640 | tf_op jit(solution)/shard_map/all_to_all | solution.py:53
  342.1 6.7 %multiply_convert_fusion.1 = (bf16[1024,192]{0,1:T(8,128)(2,1)S(1)}, bf16[1024,192]{0,1:T(8,128)(2,1)S(1)}) fusion(f32[1024,192]{0,1:T(8,128)S(1)} %fusion.6, f32[1024,192]{0,1:T(8,128)} %fusion.9, bf16[1024,4096]{1,0:T(8,128)(2,1)} %bitcast.4, bf16[1,192,4096]{2,1,0:T(8,128)(2,1)S(1)} %copy-done), kind=kOutput, calls=%fused_computation.32 | convolution fusion | flops 1613168640 | bytes 12320768 | tf_op jit(solution)/shard_map/dot_general | solution.py:67
  348.8 8.1 %fusion.4 = f32[1024,4096]{1,0:T(8,128)} fusion(bf16[1024,192]{0,1:T(8,128)(2,1)S(1)} %get-tuple-element.6, bf16[1,2,192,4096]{3,2,1,0:T(8,128)(2,1)S(1)} %copy-done.5), kind=kOutput, calls=%fused_computation.18 | convolution fusion | flops 1610612736 | bytes 18743296 | tf_op jit(solution)/shard_map/dot_general | solution.py:70
  357.0 11.4 %add_convert_fusion = bf16[1024,4096]{1,0:T(8,128)(2,1)} fusion(f32[1024,4096]{1,0:T(8,128)} %fusion.4, bf16[1024,192]{0,1:T(8,128)(2,1)S(1)} %get-tuple-element.5, bf16[1,2,192,4096]{3,2,1,0:T(8,128)(2,1)S(1)} %copy-done.5), kind=kOutput, calls=%fused_computation.7 | convolution fusion | flops 1619001344 | bytes 27131904 | tf_op jit(solution)/shard_map/dot_general | solution.py:71
  368.4 5.4 %fusion.1 = bf16[1,1,192,4096]{3,2,1,0:T(8,128)(2,1)S(1)} fusion(bf16[1024,192]{0,1:T(8,128)(2,1)S(1)} %get-tuple-element.6, bf16[1024,4096]{1,0:T(8,128)(2,1)} %bitcast.8), kind=kOutput, calls=%fused_computation.13 | convolution fusion | flops 1611399168 | bytes 10354688 | tf_op jit(solution)/shard_map/dot_general | solution.py:86
  373.8 5.8 %fusion.2 = bf16[1,1,192,4096]{3,2,1,0:T(8,128)(2,1)S(1)} fusion(bf16[1024,192]{0,1:T(8,128)(2,1)S(1)} %get-tuple-element.5, bf16[1024,4096]{1,0:T(8,128)(2,1)} %bitcast.8), kind=kOutput, calls=%fused_computation.14 | convolution fusion | flops 1611399168 | bytes 10354688 | tf_op jit(solution)/shard_map/dot_general | solution.py:87
  379.6 2.0 pad_maximum_fusion
  382.0 5.3 %fusion.3 = bf16[1,192,4096]{2,1,0:T(8,128)(2,1)S(1)} fusion(bf16[1024,4096]{1,0:T(8,128)(2,1)} %bitcast.4, f32[1024,192]{0,1:T(8,128)S(1)} %copy-done.8, f32[1024,192]{0,1:T(8,128)S(1)} %fusion.6), kind=kOutput, calls=%fused_computation.15 | convolution fusion | flops 1612578816 | bytes 11534336 | tf_op jit(solution)/shard_map/dot_general | solution.py:90
  387.3 3.6 collective-permute-start.1
  391.0 92.2 %collective-permute-done.1 = bf16[1,192,4096]{2,1,0:T(8,128)(2,1)S(1)} collective-permute-done((bf16[1,192,4096]{2,1,0:T(8,128)(2,1)S(1)}, bf16[1,192,4096]{2,1,0:T(8,128)(2,1)S(1)}, u32[]{:S(2)}, u32[]{:S(2)}) %collective-permute-start.1) | collective-permute-done | bytes 1572896 | tf_op jit(solution)/shard_map/ppermute | solution.py:20
  483.2 1.7 add_convert_fusion.2
  484.9 8.8 %all-to-all-start.3 = ((bf16[16,64,512]{2,1,0:T(8,128)(2,1)}), bf16[16,64,512]{2,1,0:T(8,128)(2,1)S(1)}, u32[]{:S(2)}, u32[]{:S(2)}) async-start(bf16[16,64,512]{2,1,0:T(8,128)(2,1)} %reduce-scatter.2.cloned.1.call-done), calls=%async_computation.4 | async-start | bytes 2097152 | tf_op jit(solution)/shard_map/all_to_all | solution.py:78
  493.7 5.8 %add_convert_fusion.1 = bf16[1,2,192,4096]{3,2,1,0:T(8,128)(2,1)} fusion(bf16[1,2,192,4096]{3,2,1,0:T(8,128)(2,1)} %collective-permute-done, bf16[1,1,192,4096]{3,2,1,0:T(8,128)(2,1)} %copy-done.2, bf16[1,1,192,4096]{3,2,1,0:T(8,128)(2,1)} %copy-done.1), kind=kLoop, calls=%fused_computation.9 | loop fusion | flops 7864320 | bytes 9437184 | tf_op jit(solution)/shard_map/convert_element_type | solution.py:95
  499.5 7.9 %all-to-all-done.3 = bf16[16,64,512]{2,1,0:T(8,128)(2,1)S(1)} async-done(((bf16[16,64,512]{2,1,0:T(8,128)(2,1)}), bf16[16,64,512]{2,1,0:T(8,128)(2,1)S(1)}, u32[]{:S(2)}, u32[]{:S(2)}) %all-to-all-start.3) | async-done | bytes 1048608 | tf_op jit(solution)/shard_map/all_to_all | solution.py:78
  507.4 2.0 gather_fusion.3
  509.5 1.3 reduce_sum.25
  (56 shorter events, 6.2 us)
Async XLA Ops:
  7.2 334.9 %copy-start = (bf16[1,192,4096]{2,1,0:T(8,128)(2,1)S(1)}, bf16[1,192,4096]{2,1,0:T(8,128)(2,1)}, u32[]{:S(2)}) copy-start(bf16[1,192,4096]{2,1,0:T(8,128)(2,1)} %param.11) | copy-start | bytes 4718596
  8.3 6.4 %copy-start.6 = (s32[128,4]{0,1:T(4,128)S(1)}, s32[128,4]{0,1:T(4,128)}, u32[]{:S(2)}) copy-start(s32[128,4]{0,1:T(4,128)} %param.8) | copy-start | bytes 6148
  8.4 8.3 %copy-start.7 = (bf16[128,4]{0,1:T(4,128)(2,1)S(1)}, bf16[128,4]{0,1:T(4,128)(2,1)}, u32[]{:S(2)}) copy-start(bf16[128,4]{0,1:T(4,128)(2,1)} %param.9) | copy-start | bytes 3076
  9.9 17.6 %all-to-all-start.1 = ((bf16[128,8,512]{2,0,1:T(8,128)(2,1)}), bf16[128,8,512]{2,0,1:T(8,128)(2,1)S(1)}, u32[]{:S(2)}, u32[]{:S(2)}) async-start(bf16[128,8,512]{2,0,1:T(8,128)(2,1)} %copy.33), calls=%async_computation.1 | async-start | bytes 2097152 | tf_op jit(solution)/shard_map/all_to_all | solution.py:9
  27.5 1.0 copy-start.3
  44.8 155.2 %all-to-all-start.2 = ((bf16[16,64,4096]{2,1,0:T(8,128)(2,1)}), bf16[16,64,4096]{2,1,0:T(8,128)(2,1)}, u32[]{:S(2)}, u32[]{:S(2)}) async-start(bf16[16,64,4096]{2,1,0:T(8,128)(2,1)} %broadcast_select_fusion), calls=%async_computation.2 | async-start | bytes 16777216 | tf_op jit(solution)/shard_map/all_to_all | solution.py:52
  52.7 26.8 %all-gather.2.cloned.1.call-start = ((), (), s32[]{:S(2)}) async-start(), calls=%async_computation.5 | async-start | bytes 1179648 | tf_op jit(solution)/shard_map/all_gather | solution.py:45
  200.0 142.1 %all-to-all-start = ((bf16[16,64,4096]{2,1,0:T(8,128)(2,1)}), bf16[16,64,4096]{2,1,0:T(8,128)(2,1)}, u32[]{:S(2)}, u32[]{:S(2)}) async-start(bf16[16,64,4096]{2,1,0:T(8,128)(2,1)} %fusion), calls=%async_computation | async-start | bytes 16777216 | tf_op jit(solution)/shard_map/all_to_all | solution.py:53
  208.4 276.5 %reduce-scatter.2.cloned.1.call-start = ((), (), s32[]{:S(2)}) async-start(), calls=%async_computation.6 | async-start | bytes 9437184 | tf_op jit(solution)/shard_map/reduce_scatter | solution.py:72
  208.6 6.9 %copy-start.4 = (bf16[1,2,192,4096]{3,2,1,0:T(8,128)(2,1)S(1)}, bf16[1,2,192,4096]{3,2,1,0:T(8,128)(2,1)}, u32[]{:S(2)}) copy-start(bf16[1,2,192,4096]{3,2,1,0:T(8,128)(2,1)} %param.10) | copy-start | bytes 9437188
  342.1 6.7 %copy-start.5 = (bf16[1,2,192,4096]{3,2,1,0:T(8,128)(2,1)S(1)}, bf16[1,2,192,4096]{3,2,1,0:T(8,128)(2,1)}, u32[]{:S(2)}) copy-start(bf16[1,2,192,4096]{3,2,1,0:T(8,128)(2,1)} %param.10) | copy-start | bytes 9437188
  373.8 5.8 %copy-start.1 = (bf16[1,1,192,4096]{3,2,1,0:T(8,128)(2,1)}, bf16[1,1,192,4096]{3,2,1,0:T(8,128)(2,1)S(1)}, u32[]{:S(2)}) copy-start(bf16[1,1,192,4096]{3,2,1,0:T(8,128)(2,1)S(1)} %fusion.1) | copy-start | bytes 4718596
  379.6 2.4 copy-start.2
  379.6 2.4 copy-start.8
  382.0 111.7 %collective-permute-start = (bf16[1,2,192,4096]{3,2,1,0:T(8,128)(2,1)}, bf16[1,2,192,4096]{3,2,1,0:T(8,128)(2,1)}, u32[]{:S(2)}, u32[]{:S(2)}) collective-permute-start(bf16[1,2,192,4096]{3,2,1,0:T(8,128)(2,1)} %pad_maximum_fusion), channel_id=1, source_target_pairs={{0,64},{64,0},{8,72},{72,8},{16,80},{80,16},{24,88},{88,24},{32,96... | collective-permute-start | bytes 9437192 | tf_op jit(solution)/shard_map/ppermute | solution.py:20
  387.3 95.8 %collective-permute-start.1 = (bf16[1,192,4096]{2,1,0:T(8,128)(2,1)S(1)}, bf16[1,192,4096]{2,1,0:T(8,128)(2,1)S(1)}, u32[]{:S(2)}, u32[]{:S(2)}) collective-permute-start(bf16[1,192,4096]{2,1,0:T(8,128)(2,1)S(1)} %fusion.3), channel_id=1, source_target_pairs={{0,64},{64,0},{8,72},{72,8},{16,80},{80,16},{24,88},{88,24},{32,96... | collective-permute-start | bytes 4718600 | tf_op jit(solution)/shard_map/ppermute | solution.py:20
  484.9 22.5 %all-to-all-start.3 = ((bf16[16,64,512]{2,1,0:T(8,128)(2,1)}), bf16[16,64,512]{2,1,0:T(8,128)(2,1)S(1)}, u32[]{:S(2)}, u32[]{:S(2)}) async-start(bf16[16,64,512]{2,1,0:T(8,128)(2,1)} %reduce-scatter.2.cloned.1.call-done), calls=%async_computation.4 | async-start | bytes 2097152 | tf_op jit(solution)/shard_map/all_to_all | solution.py:78
Sparse Core Ops, SparseCore 0:
  55.3 24.2 all-gather.1
  368.5 53.7 reduce-scatter.1
